TPU v7x, 32 devices: a whole 2x2x4 slice. The times are simulated.
32 devices in a mesh: section: 4 (over y, core), seq: 8 (over z, x).
Axes of the slice: x: 2, y: 2, z: 4, core: 2. Of those that a mesh axis runs over, the one named last changes fastest.
Arguments:
- hidden: bfloat16 [2, 1024, 4096], P(None, 'seq'), may hold values from -6 to 6
- queries: bfloat16 [4, 2, 1024, 4096], P('section', None, 'seq'), may hold values from -6 to 6
- gain: float32 [4, 4096], P('section'), may hold values from 0.5 to 2
- key_weight: bfloat16 [4, 4096, 512], P('section'), may hold values from -1 to 1
- value_weight: bfloat16 [4, 4096, 512], P('section'), may hold values from -0.09375 to 0.09375
- tree_ids: int32 [2, 1024], replicated, may hold values from 0 to 3, as said below
- branch_ids: int32 [2, 1024], replicated, may hold values from 0 to 2, as said below
- span_order: int32 [2, 16], replicated, may hold values from 0 to 15, each once within a row
Outputs:
- layer_out: bfloat16 [4, 2, 1024, 4096], P('section', None, 'seq')
Inputs may be any that keep to these rules, and one draw needn't show every extreme that they name: `tree_ids`: in each microbatch nondecreasing along the packed positions, every value of 0 to 3 present, each tree a multiple of 16 positions long. `branch_ids`: within each tree the prompt, chosen and rejected positions come in that order, each branch one position or more. `span_order`: each row is a permutation of 0 to 15.
All inputs are finite; a program needn't handle non-finite values.
Results may differ from a plain program's by a relative error of at most 0.02.
Values may be sent and summed in bfloat16 or wider, within the bound.
A program may use at most 128 MiB of HBM per device.

v0:
```python
import math

import jax
import jax.numpy as jnp
from jax import lax
from jax.sharding import PartitionSpec as P

HQ = 32
HK = 4
HD = 128
SPAN = 64


rope_base = 500000.0


def from_behind(value, axis, by):
    size = lax.axis_size(axis)
    pairs = [(i, i + by) for i in range(size) if 0 <= i + by < size]
    return lax.ppermute(value, axis, pairs)


def frequencies():
    exponent = jnp.arange(HD // 2, dtype=jnp.float32) * (2.0 / HD)
    return jnp.power(jnp.float32(rope_base), -exponent)


def rotate(vectors, angles):
    half_dim = vectors.shape[-1] // 2
    cosine = jnp.cos(angles)[..., None, :]
    sine_part = jnp.sin(angles)[..., None, :]
    lower_half = vectors[..., :half_dim]
    upper_half = vectors[..., half_dim:]
    return jnp.concatenate(
        [
            lower_half * cosine - upper_half * sine_part,
            upper_half * cosine + lower_half * sine_part,
        ],
        axis=-1,
    )


def tree_positions(tree_ids, branch_ids):
    positions = jnp.arange(tree_ids.shape[1], dtype=jnp.int32)[None, :]
    opening = jnp.concatenate(
        [jnp.ones_like(tree_ids[:, :1]), (tree_ids[:, 1:] != tree_ids[:, :-1]).astype(jnp.int32)],
        axis=1,
    )
    starts = lax.cummax(jnp.where(opening > 0, positions, 0), axis=1)
    chosen = (branch_ids == 1).astype(jnp.int32)
    counted = jnp.cumsum(chosen, axis=1, dtype=jnp.int32)
    before = jnp.take_along_axis(counted - chosen, starts, axis=1)
    skipped = jnp.where(branch_ids == 2, counted - before, 0)
    return positions - starts - skipped


def local(hidden, queries, gain, key_weight, value_weight, tree_ids, branch_ids, span_order):
    section_id = lax.axis_index("section")
    shard_id = lax.axis_index("seq")
    section_count = lax.axis_size("section")
    micro_count, row_count, model_width = hidden.shape
    seq_len = tree_ids.shape[1]
    per_pass = 1
    ratio = HQ // HK
    scale = 1.0 / math.sqrt(HD)
    rotary_all = tree_positions(tree_ids, branch_ids)
    stored_ids = jnp.arange(seq_len, dtype=jnp.int32)
    packed_all = jnp.take(span_order, stored_ids // SPAN, axis=1) * SPAN + stored_ids % SPAN
    inverse = frequencies()
    gain_row = gain[0]
    key_mat = key_weight[0]
    value_mat = value_weight[0]

    def run_layer(current, first_mb, active):
        packed = lax.dynamic_slice_in_dim(packed_all, first_mb, per_pass, 0)
        trees = lax.dynamic_slice_in_dim(tree_ids, first_mb, per_pass, 0)
        branches = lax.dynamic_slice_in_dim(branch_ids, first_mb, per_pass, 0)
        rotary = lax.dynamic_slice_in_dim(rotary_all, first_mb, per_pass, 0)
        own_packed = lax.dynamic_slice_in_dim(packed, shard_id * row_count, row_count, 1)
        own_tree = jnp.take_along_axis(trees, own_packed, axis=1)
        own_branch = jnp.take_along_axis(branches, own_packed, axis=1)
        own_angles = (
            jnp.take_along_axis(rotary, own_packed, axis=1).astype(jnp.float32)[..., None] * inverse
        )
        widened = current.astype(jnp.float32)
        norm_scale = lax.rsqrt(jnp.mean(widened * widened, axis=-1, keepdims=True) + 1e-05)
        normed = (widened * norm_scale * gain_row).astype(jnp.bfloat16)
        flat = normed.reshape(per_pass * row_count, model_width)
        key_proj = jnp.dot(flat, key_mat, preferred_element_type=jnp.float32).reshape(
            per_pass, row_count, HK, HD
        )
        key_rows = (
            rotate(key_proj, own_angles).astype(jnp.bfloat16).reshape(per_pass, row_count, HK * HD)
        )
        value_rows = (
            jnp.dot(flat, value_mat, preferred_element_type=jnp.float32)
            .astype(jnp.bfloat16)
            .reshape(per_pass, row_count, HK * HD)
        )
        query_local = lax.dynamic_slice_in_dim(queries[0], first_mb, per_pass, 0)
        turned = rotate(
            query_local.astype(jnp.float32).reshape(per_pass, row_count, HQ, HD), own_angles
        ).astype(jnp.bfloat16)
        grouped = turned.reshape(per_pass, row_count, HK, ratio, HD)
        start_top = jnp.full((per_pass, HK, ratio, row_count), -jnp.inf, jnp.float32)
        start_sum = jnp.zeros((per_pass, HK, ratio, row_count), jnp.float32)
        start_acc = jnp.zeros((per_pass, HK, ratio, row_count, HD), jnp.float32)
        key_piece = lax.all_gather(key_rows, "seq", axis=1, tiled=True)
        value_piece = lax.all_gather(value_rows, "seq", axis=1, tiled=True)
        piece_len = key_piece.shape[1]
        block_len = math.gcd(piece_len, 512)

        def update(inner, operands):
            row_top, denominator, accum = inner
            key_blk, value_blk, allowed = operands
            scores = (
                jnp.einsum(
                    "grkhd,gskd->gkhrs",
                    grouped,
                    key_blk.reshape(per_pass, block_len, HK, HD),
                    preferred_element_type=jnp.float32,
                )
                * scale
            )
            masked = jnp.where(allowed[:, None, None], scores, -jnp.inf)
            new_top = jnp.maximum(row_top, jnp.max(masked, axis=-1))
            safe_top = jnp.where(jnp.isfinite(new_top), new_top, 0.0)
            weights = jnp.exp(masked - safe_top[..., None])
            rescale = jnp.exp(row_top - safe_top)
            denominator = denominator * rescale + jnp.sum(weights, axis=-1)
            accum = accum * rescale[..., None] + jnp.einsum(
                "gkhrs,gskd->gkhrd",
                weights.astype(jnp.bfloat16),
                value_blk.reshape(per_pass, block_len, HK, HD),
                preferred_element_type=jnp.float32,
            )
            return (new_top, denominator, accum)

        def step(block_id, inner):
            begin = block_id * block_len
            key_blk = lax.dynamic_slice_in_dim(key_piece, begin, block_len, 1)
            value_blk = lax.dynamic_slice_in_dim(value_piece, begin, block_len, 1)
            key_packed = lax.dynamic_slice_in_dim(packed, begin, block_len, 1)
            key_tree = jnp.take_along_axis(trees, key_packed, axis=1)
            key_branch = jnp.take_along_axis(branches, key_packed, axis=1)
            allowed = (
                (own_tree[:, :, None] == key_tree[:, None, :])
                & (key_packed[:, None, :] <= own_packed[:, :, None])
                & (
                    (key_branch[:, None, :] == 0)
                    | (key_branch[:, None, :] == own_branch[:, :, None])
                )
            )
            operands = (key_blk, value_blk, allowed)
            return update(inner, operands)

        def sweep(inner):
            return lax.fori_loop(0, piece_len // block_len, step, inner)

        row_top, denominator, accum = lax.cond(
            active, sweep, lambda inner: inner, (start_top, start_sum, start_acc)
        )
        safe_sum = jnp.where(denominator > 0.0, denominator, 1.0)
        attended = (
            (accum / safe_sum[..., None])
            .transpose(0, 3, 1, 2, 4)
            .reshape(per_pass, row_count, HQ * HD)
            .astype(jnp.bfloat16)
        )
        return (widened + attended.astype(jnp.float32)).astype(jnp.bfloat16)

    tick_count = section_count + micro_count // per_pass - 1

    def advance(step_id, state_pair):
        previous, outputs = state_pair
        incoming = from_behind(previous, "section", 1)
        first_mb = (step_id - section_id) * per_pass
        active = (first_mb >= 0) & (first_mb < micro_count)
        start_at = jnp.clip(first_mb, 0, micro_count - per_pass)
        entering = lax.dynamic_slice_in_dim(hidden, start_at, per_pass, 0)
        current = jnp.where(section_id == 0, entering, incoming)
        computed = run_layer(current, start_at, active)
        result = jnp.where(active, computed, jnp.zeros_like(computed))
        stored = lax.dynamic_update_slice_in_dim(outputs, result, start_at, 0)
        outputs = jnp.where(active, stored, outputs)
        return (result, outputs)

    empty_pass = jnp.zeros((per_pass, row_count, model_width), jnp.bfloat16)
    empty_out = jnp.zeros((micro_count, row_count, model_width), jnp.bfloat16)
    final_pass, outputs = lax.fori_loop(0, tick_count, advance, (empty_pass, empty_out))
    return outputs[None]


def solution(mesh):
    placed = (
        P(None, "seq", None),
        P("section", None, "seq", None),
        P("section", None),
        P("section", None, None),
        P("section", None, None),
        P(),
        P(),
        P(),
    )
    return jax.shard_map(
        local,
        mesh=mesh,
        in_specs=placed,
        out_specs=P("section", None, "seq", None),
        check_vma=False,
    )
```

profile of v0, /device:TPU:29, one launch (start us, length us, event | category | flops | bytes accessed | tf_op | source)
XLA Modules:
  0.0 831.5 jit_solution(15143420535442001933)
XLA Ops:
  6.5 6.4 copy.28
  15.3 17.7 %gather_fusion.6 = s32[2048]{0:T(1024)S(1)} fusion(s32[2,1024]{1,0:T(2,128)S(1)} %bitcast_subtract_fusion, s32[2048]{0:T(1024)S(1)} %bitcast.246), kind=kCustom, calls=%fused_computation.6 | custom fusion | bytes 32768 | tf_op jit(solution)/shard_map/jit(take_along_axis)/gather | solution.py:52
  33.3 2.8 gather_fusion.5
  38.2 786.5 %while.41 = (s32[]{:T(128)}, bf16[1,128,4096]{2,1,0:T(8,128)(2,1)}, bf16[2,128,4096]{2,1,0:T(8,128)(2,1)}, s32[]{:T(128)}, pred[]{:T(512)}, /*index=5*/bf16[2,12...) while((s32[]{:T(128)}, bf16[1,128,4096]{2,1,0:T(8,128)(2,1)}, ...), condition=%wide.region_12.15_spmd.clone, body=%wide.region_4.14_spmd.clone.sunk | while | flops 2188912640 | bytes 124534680 | solution.py:190
  44.8 3.9 convolution_bitcast_fusion.2
  49.4 3.7 convolution_convert_fusion.2
  56.7 2.5 subtract_convert_fusion.5
  59.8 38.3 %all-gather.7.cloned.1.call-done = bf16[1,1024,512]{1,2,0:T(8,128)(2,1)} async-done(((bf16[1,128,512]{1,2,0:T(8,128)(2,1)}), bf16[1,1024,512]{1,2,0:T(8,128)(2,1)}) %all-gather.7.cloned.1.call-update) | async-done | bytes 1048592 | tf_op jit(solution)/shard_map/while/body/eval_jaxpr/all_gather | solution.py:108
  98.1 41.3 %all-gather.9.cloned.1.call-done = bf16[1024,512]{1,0:T(8,128)(2,1)} async-done(((bf16[128,512]{1,0:T(8,128)(2,1)}), bf16[1024,512]{1,0:T(8,128)(2,1)}) %all-gather.9.cloned.1.call-update) | async-done | bytes 1048592 | tf_op jit(solution)/shard_map/while/body/eval_jaxpr/all_gather | solution.py:109
  144.3 2.6 copy.73
  148.7 3.1 select_dynamic-update-slice_fusion.2
  155.7 4.0 collective-permute-done
  161.4 3.9 convolution_bitcast_fusion.2
  166.1 3.7 convolution_convert_fusion.2
  173.4 2.5 subtract_convert_fusion.5
  176.4 69.5 %all-gather.7.cloned.1.call-done = bf16[1,1024,512]{1,2,0:T(8,128)(2,1)} async-done(((bf16[1,128,512]{1,2,0:T(8,128)(2,1)}), bf16[1,1024,512]{1,2,0:T(8,128)(2,1)}) %all-gather.7.cloned.1.call-update) | async-done | bytes 1048592 | tf_op jit(solution)/shard_map/while/body/eval_jaxpr/all_gather | solution.py:108
  245.9 41.2 %all-gather.9.cloned.1.call-done = bf16[1024,512]{1,0:T(8,128)(2,1)} async-done(((bf16[128,512]{1,0:T(8,128)(2,1)}), bf16[1024,512]{1,0:T(8,128)(2,1)}) %all-gather.9.cloned.1.call-update) | async-done | bytes 1048592 | tf_op jit(solution)/shard_map/while/body/eval_jaxpr/all_gather | solution.py:109
  292.0 2.6 copy.73
  296.4 3.1 select_dynamic-update-slice_fusion.2
  303.4 4.0 collective-permute-done
  309.1 3.9 convolution_bitcast_fusion.2
  313.8 3.8 convolution_convert_fusion.2
  321.1 2.5 subtract_convert_fusion.5
  324.1 79.3 %all-gather.7.cloned.1.call-done = bf16[1,1024,512]{1,2,0:T(8,128)(2,1)} async-done(((bf16[1,128,512]{1,2,0:T(8,128)(2,1)}), bf16[1,1024,512]{1,2,0:T(8,128)(2,1)}) %all-gather.7.cloned.1.call-update) | async-done | bytes 1048592 | tf_op jit(solution)/shard_map/while/body/eval_jaxpr/all_gather | solution.py:108
  403.4 41.2 %all-gather.9.cloned.1.call-done = bf16[1024,512]{1,0:T(8,128)(2,1)} async-done(((bf16[128,512]{1,0:T(8,128)(2,1)}), bf16[1024,512]{1,0:T(8,128)(2,1)}) %all-gather.9.cloned.1.call-update) | async-done | bytes 1048592 | tf_op jit(solution)/shard_map/while/body/eval_jaxpr/all_gather | solution.py:109
  449.5 2.6 copy.73
  453.9 3.1 select_dynamic-update-slice_fusion.2
  460.9 49.5 %collective-permute-done = bf16[1,128,4096]{2,1,0:T(8,128)(2,1)S(1)} collective-permute-done((bf16[1,128,4096]{2,1,0:T(8,128)(2,1)S(1)}, bf16[1,128,4096]{2,1,0:T(8,128)(2,1)S(1)}, u32[]{:S(2)}, u32[]{:S(2)}) %collective-permute-start) | collective-permute-done | bytes 1048608 | tf_op jit(solution)/shard_map/while/body/eval_jaxpr/ppermute | solution.py:20
  512.1 3.9 convolution_bitcast_fusion.2
  516.8 3.8 convolution_convert_fusion.2
  524.1 2.5 subtract_convert_fusion.5
  527.1 37.4 %all-gather.7.cloned.1.call-done = bf16[1,1024,512]{1,2,0:T(8,128)(2,1)} async-done(((bf16[1,128,512]{1,2,0:T(8,128)(2,1)}), bf16[1,1024,512]{1,2,0:T(8,128)(2,1)}) %all-gather.7.cloned.1.call-update) | async-done | bytes 1048592 | tf_op jit(solution)/shard_map/while/body/eval_jaxpr/all_gather | solution.py:108
  564.5 41.3 %all-gather.9.cloned.1.call-done = bf16[1024,512]{1,0:T(8,128)(2,1)} async-done(((bf16[128,512]{1,0:T(8,128)(2,1)}), bf16[1024,512]{1,0:T(8,128)(2,1)}) %all-gather.9.cloned.1.call-update) | async-done | bytes 1048592 | tf_op jit(solution)/shard_map/while/body/eval_jaxpr/all_gather | solution.py:109
  605.8 47.6 %conditional.3 = (f32[1,4,8,128]{3,2,1,0:T(8,128)}, f32[1,4,8,128,128]{4,3,2,1,0:T(8,128)}) conditional(s32[]{:T(128)} %convert_element_type.273, () %tuple.129, (s32[2,1024]{1,0:T(2,128)S(1)}, s32[]{:T(128)}, pred[1,128]{1,0:T(4,128)(4,1)S(1)}, s32[1,1024]{1,0:T(1,128)S(1)}, s32[1,128]{1,0:T(1,128)S(1)}, /*index=5*/s32[1,1024]{1,0:T(1,128)S(1)}, ...), branch_computations={%region_6.7_spmd, %region_7.13_spmd.clone} | conditional | flops 1098833152 | bytes 43605192 | solution.py:160
  605.9 47.6 %while.40 = (s32[]{:T(128)}, f32[1,4,8,128]{3,2,1,0:T(8,128)S(1)}, f32[1,4,8,128]{3,2,1,0:T(8,128)}, f32[1,4,8,128,128]{4,3,2,1,0:T(8,128)}, s32[1,128]{1,0:T(1,...) while((s32[]{:T(128)}, f32[1,4,8,128]{3,2,1,0:T(8,128)S(1)}, ...), condition=%wide.region_11.12_spmd.clone, body=%wide.region_8.11_spmd.clone.sunk | while | flops 1098832896 | bytes 43594528 | solution.py:158
  605.9 2.3 gather_fusion
  608.2 2.3 gather_fusion.1
  610.9 4.7 fusion.86
  615.6 5.2 fusion.89
  621.8 7.3 bitcast_add_fusion.5
  629.1 2.3 gather_fusion
  631.3 2.3 gather_fusion.1
  634.1 4.7 fusion.86
  638.8 5.2 fusion.89
  645.6 7.9 bitcast_add_fusion.5
  656.1 2.6 copy.73
  660.6 3.1 select_dynamic-update-slice_fusion.2
  667.6 4.0 collective-permute-done
  673.3 3.9 convolution_bitcast_fusion.2
  678.0 3.7 convolution_convert_fusion.2
  685.3 2.5 subtract_convert_fusion.5
  688.3 37.4 %all-gather.7.cloned.1.call-done = bf16[1,1024,512]{1,2,0:T(8,128)(2,1)} async-done(((bf16[1,128,512]{1,2,0:T(8,128)(2,1)}), bf16[1,1024,512]{1,2,0:T(8,128)(2,1)}) %all-gather.7.cloned.1.call-update) | async-done | bytes 1048592 | tf_op jit(solution)/shard_map/while/body/eval_jaxpr/all_gather | solution.py:108
  725.7 41.2 %all-gather.9.cloned.1.call-done = bf16[1024,512]{1,0:T(8,128)(2,1)} async-done(((bf16[128,512]{1,0:T(8,128)(2,1)}), bf16[1024,512]{1,0:T(8,128)(2,1)}) %all-gather.9.cloned.1.call-update) | async-done | bytes 1048592 | tf_op jit(solution)/shard_map/while/body/eval_jaxpr/all_gather | solution.py:109
  766.9 47.6 %conditional.3 = (f32[1,4,8,128]{3,2,1,0:T(8,128)}, f32[1,4,8,128,128]{4,3,2,1,0:T(8,128)}) conditional(s32[]{:T(128)} %convert_element_type.273, () %tuple.129, (s32[2,1024]{1,0:T(2,128)S(1)}, s32[]{:T(128)}, pred[1,128]{1,0:T(4,128)(4,1)S(1)}, s32[1,1024]{1,0:T(1,128)S(1)}, s32[1,128]{1,0:T(1,128)S(1)}, /*index=5*/s32[1,1024]{1,0:T(1,128)S(1)}, ...), branch_computations={%region_6.7_spmd, %region_7.13_spmd.clone} | conditional | flops 1098833152 | bytes 43605192 | solution.py:160
  766.9 47.6 %while.40 = (s32[]{:T(128)}, f32[1,4,8,128]{3,2,1,0:T(8,128)S(1)}, f32[1,4,8,128]{3,2,1,0:T(8,128)}, f32[1,4,8,128,128]{4,3,2,1,0:T(8,128)}, s32[1,128]{1,0:T(1,...) while((s32[]{:T(128)}, f32[1,4,8,128]{3,2,1,0:T(8,128)S(1)}, ...), condition=%wide.region_11.12_spmd.clone, body=%wide.region_8.11_spmd.clone.sunk | while | flops 1098832896 | bytes 43594528 | solution.py:158
  767.0 2.3 gather_fusion
  772.0 4.7 fusion.86
  776.7 5.2 fusion.89
  782.8 7.3 bitcast_add_fusion.5
  795.1 4.7 fusion.86
  799.8 5.2 fusion.89
  806.6 7.9 bitcast_add_fusion.5
  817.2 2.6 copy.73
  821.6 3.1 select_dynamic-update-slice_fusion.2
  (299 shorter events, 106.4 us)
Async XLA Ops:
  6.5 6.4 copy-start.5
  6.5 7.5 copy-start.6
  15.3 17.8 %copy-start.7 = (s32[2,16]{1,0:T(2,128)S(1)}, s32[2,16]{1,0:T(2,128)}, u32[]{:S(2)}) copy-start(s32[2,16]{1,0:T(2,128)} %param.25) | copy-start | bytes 388
  33.0 5.2 copy-start.8
  38.2 59.9 %all-gather.7.cloned.1.call-start = ((), (), s32[]{:S(2)}) async-start(), calls=%async_computation | async-start | bytes 1179648 | tf_op jit(solution)/shard_map/while/body/eval_jaxpr/all_gather | solution.py:108
  38.3 4.7 collective-permute-start
  44.7 4.7 copy-start.2
  49.4 90.1 %all-gather.9.cloned.1.call-start = ((), (), s32[]{:S(2)}) async-start(), calls=%async_computation.1 | async-start | bytes 1179648 | tf_op jit(solution)/shard_map/while/body/eval_jaxpr/all_gather | solution.py:109
  49.4 4.0 copy-start.4
  146.8 1.9 copy-start.3
  151.8 94.1 %all-gather.7.cloned.1.call-start = ((), (), s32[]{:S(2)}) async-start(), calls=%async_computation | async-start | bytes 1179648 | tf_op jit(solution)/shard_map/while/body/eval_jaxpr/all_gather | solution.py:108
  153.1 6.6 collective-permute-start
  161.4 4.7 copy-start.2
  166.0 121.1 %all-gather.9.cloned.1.call-start = ((), (), s32[]{:S(2)}) async-start(), calls=%async_computation.1 | async-start | bytes 1179648 | tf_op jit(solution)/shard_map/while/body/eval_jaxpr/all_gather | solution.py:109
  166.1 4.0 copy-start.4
  294.5 1.9 copy-start.3
  299.4 104.0 %all-gather.7.cloned.1.call-start = ((), (), s32[]{:S(2)}) async-start(), calls=%async_computation | async-start | bytes 1179648 | tf_op jit(solution)/shard_map/while/body/eval_jaxpr/all_gather | solution.py:108
  300.7 6.6 collective-permute-start
  309.1 4.7 copy-start.2
  313.7 130.9 %all-gather.9.cloned.1.call-start = ((), (), s32[]{:S(2)}) async-start(), calls=%async_computation.1 | async-start | bytes 1179648 | tf_op jit(solution)/shard_map/while/body/eval_jaxpr/all_gather | solution.py:109
  313.8 4.0 copy-start.4
  452.0 1.9 copy-start.3
  457.0 107.5 %all-gather.7.cloned.1.call-start = ((), (), s32[]{:S(2)}) async-start(), calls=%async_computation | async-start | bytes 1179648 | tf_op jit(solution)/shard_map/while/body/eval_jaxpr/all_gather | solution.py:108
  458.3 52.1 %collective-permute-start = (bf16[1,128,4096]{2,1,0:T(8,128)(2,1)S(1)}, bf16[1,128,4096]{2,1,0:T(8,128)(2,1)S(1)}, u32[]{:S(2)}, u32[]{:S(2)}) collective-permute-start(bf16[1,128,4096]{2,1,0:T(8,128)(2,1)S(1)} %broadcast_select_fusion.7), channel_id=1, source_target_pairs={{0,8},{8,16},{16,24},{1,9},{9,17},{17,25},{2,10},{10,18},{18,26},{... | collective-permute-start | bytes 3145736 | tf_op jit(solution)/shard_map/while/body/eval_jaxpr/ppermute | solution.py:20
  512.0 4.7 copy-start.2
  516.7 89.1 %all-gather.9.cloned.1.call-start = ((), (), s32[]{:S(2)}) async-start(), calls=%async_computation.1 | async-start | bytes 1179648 | tf_op jit(solution)/shard_map/while/body/eval_jaxpr/all_gather | solution.py:109
  516.8 4.0 copy-start.4
  605.9 5.0 copy-start
  615.6 5.9 copy-start.1
  629.0 5.0 copy-start
  638.8 6.6 copy-start.1
  658.7 1.9 copy-start.3
  663.6 62.0 %all-gather.7.cloned.1.call-start = ((), (), s32[]{:S(2)}) async-start(), calls=%async_computation | async-start | bytes 1179648 | tf_op jit(solution)/shard_map/while/body/eval_jaxpr/all_gather | solution.py:108
  664.9 6.6 collective-permute-start
  673.2 4.7 copy-start.2
  677.9 89.0 %all-gather.9.cloned.1.call-start = ((), (), s32[]{:S(2)}) async-start(), calls=%async_computation.1 | async-start | bytes 1179648 | tf_op jit(solution)/shard_map/while/body/eval_jaxpr/all_gather | solution.py:109
  678.0 4.0 copy-start.4
  767.0 5.0 copy-start
  776.7 5.9 copy-start.1
  790.1 5.0 copy-start
  799.8 6.6 copy-start.1
  819.8 1.9 copy-start.3
Sparse Core Ops, SparseCore 0:
  49.5 48.5 all-gather.6
  100.2 39.1 all-gather.8
  166.1 79.7 all-gather.6
  247.9 39.1 all-gather.8
  313.8 89.5 all-gather.6
  405.4 39.1 all-gather.8
  516.8 47.6 all-gather.6
  566.6 39.1 all-gather.8
  678.0 47.6 all-gather.6
  727.7 39.1 all-gather.8
where the time goes:
time: 836 us; the launch traced here: 832 us
  waiting for transfers between devices  532 us (64%)
  local copies, waits for them, and re-layouts  98.4 us (12%)
  other arithmetic  92.3 us (11%)
  matrix products  87.1 us (10%)
  between operations  13.5 us (2%)
    all_gather x5, waiting for transfers between devices, run_layer(): key_piece = lax.all_gather(key_rows, 'seq', axis=1, tiled=True)  262 us
    all_gather x5, waiting for transfers between devices, run_layer(): value_piece = lax.all_gather(value_rows, 'seq', axis=1, tiled=True)  206 us
    ppermute x5, waiting for transfers between devices, from_behind(): return lax.ppermute(value, axis, pairs)  63.6 us
    dot_general x4, matrix products, update(): jnp.einsum('gkhrs,gskd->gkhrd', weights.astype(jnp.bfloat16), value_blk.r...  30.3 us
    convert_element_type x10, local copies, waits for them, and re-layouts, run_layer(): return (widened + attended.astype(jnp.float32)).astype(jnp.bfloat16)  22 us
    reduce_sum x4, other arithmetic, update(): denominator = denominator * rescale + jnp.sum(weights, axis=-1)  20.9 us
    dot_general x5, matrix products, run_layer(): jnp.dot(flat, key_mat, preferred_element_type=jnp.float32)  19.5 us
    dot_general x5, matrix products, run_layer(): jnp.dot(flat, value_mat, preferred_element_type=jnp.float32)  18.7 us
  transfers between devices with their start and end apart: 15, of which 15 were waited for; matrix products, arithmetic and copies ran while one was open for 7% of the time, Pallas kernels for 0%

commit v1 on v0

v1 whole, which is shorter than its diff:
```python
import functools
import math

import jax
import jax.numpy as jnp
from jax import lax
from jax.experimental import pallas as pl
from jax.experimental.pallas import tpu as pltpu
from jax.sharding import PartitionSpec as P

HQ = 32
HK = 4
HD = 128
SPAN = 64
RATIO = HQ // HK
TILE_HEADS = 4
HIDDEN_AWAY = -1e30
ROPE_BASE = 500000.0
MESH = pl.DeviceIdType.MESH


def kernel(
    sections,
    z_size,
    x_size,
    span_ref,
    rows_ref,
    inverse_ref,
    gain_ref,
    hidden_ref,
    queries_ref,
    key_ref,
    value_ref,
    out_ref,
    state,
    raw,
    turned,
    key_mat,
    value_mat,
    total,
    cosine,
    sine,
    bias,
    kv,
    values,
    result,
    state_sem,
    raw_sem,
    weight_sem,
    next_sem,
    out_sem,
    own_sem,
    pass_sem,
    kv_sem,
):
    section = lax.axis_index("section")
    me = lax.axis_index("seq")
    z = me // x_size
    x = me % x_size
    micro, _, rows, chunk = state.shape
    seq_len = rows_ref.shape[2]
    spans = rows // SPAN
    width = HK * chunk

    @pl.when(section == 0)
    def _():
        for mb in range(micro):
            for c in range(HK):
                pltpu.make_async_copy(
                    hidden_ref.at[mb, :, pl.ds(c * chunk, chunk)],
                    state.at[mb, c],
                    state_sem.at[mb, c],
                ).start()

    def weight_copies(c):
        part = pl.ds(c * chunk, chunk)
        return (
            pltpu.make_async_copy(key_ref.at[0, part], key_mat.at[part], weight_sem.at[0, c]),
            pltpu.make_async_copy(value_ref.at[0, part], value_mat.at[part], weight_sem.at[1, c]),
        )

    for c in range(HK):
        for copy in weight_copies(c):
            copy.start()

    def raw_copy(mb):
        return pltpu.make_async_copy(queries_ref.at[0, mb], raw.at[mb], raw_sem.at[mb])

    for mb in range(micro):
        raw_copy(mb).start()

    barrier = pltpu.get_barrier_semaphore()
    z_peers = [lax.rem(z + d, z_size) * x_size + x for d in range(1, z_size)]
    x_peers = [z * x_size + lax.rem(x + d, x_size) for d in range(1, x_size)]
    for peer in z_peers + x_peers:
        pl.semaphore_signal(barrier, inc=1, device_id=(section, peer), device_id_type=MESH)

    @pl.when(section > 0)
    def _():
        pl.semaphore_signal(barrier, inc=1, device_id=(section - 1, me), device_id_type=MESH)

    @pl.when(section < sections - 1)
    def _():
        pl.semaphore_signal(barrier, inc=1, device_id=(section + 1, me), device_id_type=MESH)

    at_end = (section == 0) | (section == sections - 1)
    peers = len(z_peers) + len(x_peers)

    @pl.when(at_end)
    def _():
        pl.semaphore_wait(barrier, peers + 1)

    @pl.when(jnp.logical_not(at_end))
    def _():
        pl.semaphore_wait(barrier, peers + 2)

    fold = math.log2(math.e) / math.sqrt(HD)
    place = lax.broadcasted_iota(jnp.int32, (rows, 1), 0)
    lanes = lax.broadcasted_iota(jnp.int32, (rows, HD), 1)
    ids = lax.broadcasted_iota(jnp.int32, (rows, seq_len), 1).astype(jnp.float32)

    def count(flags):
        return jnp.sum(jnp.where(flags, 1.0, 0.0), axis=1, keepdims=True)

    for mb in range(micro):
        position = place % SPAN
        for k in range(spans):
            offset = span_ref[mb, me * spans + k] * SPAN
            position = position + jnp.where(place // SPAN == k, offset, 0)
        position = position.astype(jnp.float32)
        tree_row = rows_ref[mb, 0:1, :]
        branch_row = rows_ref[mb, 1:2, :]
        packed_row = rows_ref[mb, 2:3, :]
        code_row = tree_row * 3.0 + branch_row
        here = ids == position
        code = jnp.sum(jnp.where(here, code_row, 0.0), axis=1, keepdims=True)
        tree = jnp.sum(jnp.where(here, tree_row, 0.0), axis=1, keepdims=True)
        first = tree * 3.0
        start = count(code_row < first)
        prompt_end = count(code_row < first + 1.0)
        chosen_end = count(code_row < first + 2.0)
        rejected = (code - first) > 1.5
        gap_from = jnp.where(rejected, prompt_end, 0.0)
        gap_to = jnp.where(rejected, chosen_end, 0.0)
        allowed = (
            (packed_row >= start)
            & (packed_row <= position)
            & ((packed_row < gap_from) | (packed_row >= gap_to))
        )
        bias[mb] = jnp.where(allowed, 0.0, HIDDEN_AWAY)
        angle = (position - start - (gap_to - gap_from)) * inverse_ref[...]
        cosine[mb] = jnp.cos(angle)
        turn = jnp.sin(angle)
        sine[mb] = jnp.where(lanes < HD // 2, -turn, turn)

    values[:, HD:] = jnp.ones((seq_len, HD), jnp.bfloat16)

    def project(mb, first):
        square = jnp.zeros((rows, 1), jnp.float32)
        for c in range(HK):
            if first:
                for copy in weight_copies(c):
                    copy.wait()
            pltpu.make_async_copy(state.at[mb, c], state.at[mb, c], state_sem.at[mb, c]).wait()
            part = pl.ds(c * chunk, chunk)
            wide = state[mb, c].astype(jnp.float32)
            square = square + jnp.sum(wide * wide, axis=1, keepdims=True)
            gained = (wide * gain_ref[:, part]).astype(jnp.bfloat16)
            keys = jnp.dot(gained, key_mat[part, :], preferred_element_type=jnp.float32)
            vals = jnp.dot(gained, value_mat[part, :], preferred_element_type=jnp.float32)
            if c == 0:
                total[0] = keys
                total[1] = vals
            else:
                total[0] += keys
                total[1] += vals
        norm = lax.rsqrt(square * (1.0 / width) + 1e-05)
        for g in range(HK):
            head = pl.ds(g * HD, HD)
            key = total[0, :, head] * norm
            key = key * cosine[mb] + pltpu.roll(key, HD // 2, 1) * sine[mb]
            kv[mb, g, me, :, :HD] = key.astype(jnp.bfloat16)
            kv[mb, g, me, :, HD:] = (total[1, :, head] * norm).astype(jnp.bfloat16)
            for i in range(len(z_peers) + len(x_peers)):
                own_copy(mb, g, i).start()

    def own_copy(mb, g, i):
        peer = (z_peers + x_peers)[i]
        return pltpu.make_async_remote_copy(
            src_ref=kv.at[mb, g, me],
            dst_ref=kv.at[mb, g, me],
            send_sem=own_sem.at[mb, g, i],
            recv_sem=kv_sem.at[mb, g, me],
            device_id=(section, peer),
            device_id_type=MESH,
        )

    def pass_copy(mb, g, i, j):
        return pltpu.make_async_remote_copy(
            src_ref=kv.at[mb, g, z_peers[i]],
            dst_ref=kv.at[mb, g, z_peers[i]],
            send_sem=pass_sem.at[mb, g, i, j],
            recv_sem=kv_sem.at[mb, g, z_peers[i]],
            device_id=(section, x_peers[j]),
            device_id_type=MESH,
        )

    def arrived(mb, g, slot):
        block = kv.at[mb, g, slot]
        pltpu.make_async_copy(block, block, kv_sem.at[mb, g, slot]).wait()

    def hand_on(mb, g):
        for i in range(z_size - 1):
            arrived(mb, g, z_peers[i])
            for j in range(x_size - 1):
                pass_copy(mb, g, i, j).start()

    def all_here(mb, g):
        for d in range(1, x_size):
            for e in range(z_size):
                arrived(mb, g, lax.rem(z + e, z_size) * x_size + lax.rem(x + d, x_size))

    def next_copy(mb, g):
        return pltpu.make_async_remote_copy(
            src_ref=result.at[mb, g],
            dst_ref=state.at[mb, g],
            send_sem=next_sem.at[mb, g],
            recv_sem=state_sem.at[mb, g],
            device_id=(section + 1, me),
            device_id_type=MESH,
        )

    def out_copy(mb, g):
        return pltpu.make_async_copy(
            result.at[mb, g],
            out_ref.at[0, mb, :, pl.ds(pl.multiple_of(g * chunk, chunk), chunk)],
            out_sem.at[mb, g],
        )

    def turn_queries(mb):
        raw_copy(mb).wait()
        spread = cosine[mb] * fold
        cross = sine[mb] * fold

        def group(g, carry):
            for r in range(RATIO):
                h = g * RATIO + r
                query = raw[mb, :, pl.ds(pl.multiple_of(h * HD, HD), HD)].astype(jnp.float32)
                turned[mb, h] = (query * spread + pltpu.roll(query, HD // 2, 1) * cross).astype(
                    jnp.bfloat16
                )
            return carry

        lax.fori_loop(0, HK, group, 0)

    def attend(mb):
        hand_on(mb, 0)

        def group(g, carry):
            @pl.when(g < HK - 1)
            def _():
                hand_on(mb, g + 1)

            all_here(mb, g)
            values[:, :HD] = kv[mb, g, :, :, HD:].reshape(seq_len, HD)
            for t in range(RATIO // TILE_HEADS):
                query = turned[mb, pl.ds(g * RATIO + t * TILE_HEADS, TILE_HEADS)]
                keys = kv[mb, g, :, :, :HD].reshape(seq_len, HD)
                scores = lax.dot_general(
                    query.reshape(TILE_HEADS * rows, HD),
                    keys,
                    (((1,), (1,)), ((), ())),
                    preferred_element_type=jnp.float32,
                )
                scores = scores.reshape(TILE_HEADS, rows, seq_len) + bias[mb]
                top = jnp.max(scores, axis=-1, keepdims=True)
                weights = jnp.exp2(scores - top).astype(jnp.bfloat16)
                summed = jnp.dot(
                    weights.reshape(TILE_HEADS * rows, seq_len),
                    values[...],
                    preferred_element_type=jnp.float32,
                )
                attended = (summed[:, :HD] / summed[:, HD:]).astype(jnp.bfloat16)
                for r in range(TILE_HEADS):
                    part = pl.ds((t * TILE_HEADS + r) * HD, HD)
                    result[mb, g, :, part] = (
                        state[mb, g, :, part].astype(jnp.float32)
                        + attended[r * rows : (r + 1) * rows].astype(jnp.float32)
                    ).astype(jnp.bfloat16)

            @pl.when(section < sections - 1)
            def _():
                next_copy(mb, g).start()

            out_copy(mb, g).start()
            return carry

        lax.fori_loop(0, HK, group, 0)

    @pl.when(section > 0)
    def _():
        for mb in range(micro):
            turn_queries(mb)

    project(0, True)

    @pl.when(section == 0)
    def _():
        for mb in range(1, micro):
            project(mb, False)
        for mb in range(micro):
            turn_queries(mb)

    for mb in range(micro):
        attend(mb)
        if mb + 1 < micro:

            @pl.when(section > 0)
            def _():
                project(mb + 1, False)

    def finish(g, carry):
        for mb in range(micro):
            for i in range(len(z_peers) + len(x_peers)):
                own_copy(mb, g, i).wait_send()
            for i in range(z_size - 1):
                for j in range(x_size - 1):
                    pass_copy(mb, g, i, j).wait_send()
            out_copy(mb, g).wait()

            @pl.when(section < sections - 1)
            def _():
                next_copy(mb, g).wait_send()

        return carry

    lax.fori_loop(0, HK, finish, 0)


def local(sections, z_size, x_size, hidden, queries, gain, key_weight, value_weight, tree_ids,
          branch_ids, span_order):
    micro, rows, width = hidden.shape
    seq_len = tree_ids.shape[1]
    seq = z_size * x_size
    chunk = width // HK
    within = jnp.arange(SPAN, dtype=jnp.int32)
    packed = (span_order[:, :, None] * SPAN + within).reshape(micro, seq_len)
    stacked = jnp.stack([tree_ids, branch_ids, packed], axis=1).astype(jnp.float32)
    exponent = jnp.arange(HD // 2, dtype=jnp.float32) * (2.0 / HD)
    inverse = jnp.power(jnp.float32(ROPE_BASE), -exponent)
    inverse = jnp.concatenate([inverse, inverse])[None]
    vmem = pl.BlockSpec(memory_space=pltpu.VMEM)
    anywhere = pl.BlockSpec(memory_space=pl.ANY)
    half = jnp.bfloat16
    dma = pltpu.SemaphoreType.DMA
    return pl.pallas_call(
        functools.partial(kernel, sections, z_size, x_size),
        out_shape=jax.ShapeDtypeStruct((1, micro, rows, width), half),
        in_specs=[pl.BlockSpec(memory_space=pltpu.SMEM)] + [vmem] * 3 + [anywhere] * 4,
        out_specs=anywhere,
        scratch_shapes=[
            pltpu.VMEM((micro, HK, rows, chunk), half),
            pltpu.VMEM((micro, rows, width), half),
            pltpu.VMEM((micro, HQ, rows, HD), half),
            pltpu.VMEM((width, HK * HD), half),
            pltpu.VMEM((width, HK * HD), half),
            pltpu.VMEM((2, rows, HK * HD), jnp.float32),
            pltpu.VMEM((micro, rows, HD), jnp.float32),
            pltpu.VMEM((micro, rows, HD), jnp.float32),
            pltpu.VMEM((micro, rows, seq_len), jnp.float32),
            pltpu.VMEM((micro, HK, seq, rows, 2 * HD), half),
            pltpu.VMEM((seq_len, 2 * HD), half),
            pltpu.VMEM((micro, HK, rows, chunk), half),
            dma((micro, HK)),
            dma((micro,)),
            dma((2, HK)),
            dma((micro, HK)),
            dma((micro, HK)),
            dma((micro, HK, z_size + x_size - 2)),
            dma((micro, HK, max(z_size - 1, 1), max(x_size - 1, 1))),
            dma((micro, HK, seq)),
        ],
        compiler_params=pltpu.CompilerParams(
            collective_id=0, has_side_effects=True, vmem_limit_bytes=56 * 1024 * 1024
        ),
    )(span_order, stacked, inverse, gain, hidden, queries, key_weight, value_weight)


def solution(mesh):
    seq = mesh.shape["seq"]
    z_size = math.gcd(seq, 4)
    placed = (
        P(None, "seq", None),
        P("section", None, "seq", None),
        P("section", None),
        P("section", None, None),
        P("section", None, None),
        P(),
        P(),
        P(),
    )
    return jax.shard_map(
        functools.partial(local, mesh.shape["section"], z_size, seq // z_size),
        mesh=mesh,
        in_specs=placed,
        out_specs=P("section", None, "seq", None),
        check_vma=False,
    )
```

time: 836 us -> 148 us (0.18)
  waiting for transfers between devices: 532 us -> 0 us
  Pallas kernels: 0 us -> 141 us
  local copies, waits for them, and re-layouts: 98.4 us -> 4.76 us
  other arithmetic: 92.3 us -> 1.94 us
  matrix products: 87.1 us -> 0 us
  between operations: 13.5 us -> 0.02 us
    all_gather x10 -> x0, waiting for transfers between devices: 468 us -> none  [the longest x5 262 us: run_layer(): key_piece = lax.all_gather(key_rows, 'seq', axis=1, tiled=True)]
    pallas_call x0 -> x1, Pallas kernels: none -> 141 us  [local(): pl.pallas_call(functools.partial(kernel, sections, z_size, x_size), out_s...]
    dot_general x18 -> x0, matrix products: 87.1 us -> none  [the longest x4 30.3 us: update(): jnp.einsum('gkhrs,gskd->gkhrd', weights.astype(jnp.bfloat16), value_blk.r...]
    ppermute x5 -> x0, waiting for transfers between devices: 63.6 us -> none  [from_behind(): return lax.ppermute(value, axis, pairs)]
    gather x26 -> x0, local copies, waits for them, and re-layouts: 53.4 us -> none  [the longest x2 17.7 us: tree_positions(): before = jnp.take_along_axis(counted - chosen, starts, axis=1)]
    reduce_sum x9 -> x0, other arithmetic: 29.3 us -> none  [the longest x4 20.9 us: update(): denominator = denominator * rescale + jnp.sum(weights, axis=-1)]
    convert_element_type x10 -> x0, local copies, waits for them, and re-layouts: 22 us -> none  [run_layer(): return (widened + attended.astype(jnp.float32)).astype(jnp.bfloat16)]
    select_n x17 -> x0, other arithmetic: 15.4 us -> none  [the longest x5 15.3 us: advance(): outputs = jnp.where(active, stored, outputs)]
  transfers between devices with their start and end apart: 15 -> 0, of which waited for: 15 -> 0; matrix products, arithmetic and copies ran while one was open for 7% -> 0% of each run, Pallas kernels for 0% -> 0%
where the time goes in v1:
time: 148 us; the launch traced here: 147 us
  Pallas kernels  141 us (95%)
  local copies, waits for them, and re-layouts  4.76 us (3%)
  other arithmetic  1.94 us (1%)
    pallas_call x1, Pallas kernels, local(): pl.pallas_call(functools.partial(kernel, sections, z_size, x_size), out_s...  141 us
    unnamed x1, local copies, waits for them, and re-layouts  3.13 us

profile of v1, /device:TPU:29, one launch (start us, length us, event | category | flops | bytes accessed | tf_op | source)
XLA Modules:
  0.0 147.3 jit_solution(11461333849141208642)
XLA Ops:
  0.0 0.6 maximum_bitcast_fusion.inverse_ref
  0.6 0.7 broadcast_multiply_fusion
  1.3 0.7 stack.9
  2.0 0.7 stack.10
  2.7 0.1 add.29
  2.8 0.1 add.26
  2.8 0.1 add.27
  2.9 0.6 add_convert_fusion.rows_ref
  3.6 140.6 %shard_map.82 = bf16[1,2,128,4096]{3,2,1,0:T(8,128)(2,1)} custom-call(s32[2,16]{1,0:T(2,128)} %span_ref.1, f32[2,3,1024]{2,1,0:T(4,128)} %add_convert_fusion.rows_ref, f32[1,128]{1,0:T(1,128)} %maximum_bitcast_fusion.inverse_ref, f32[1,4096]{1,0:T(1,128)} %gain_ref.1, bf16[2,128,4096]{2,1,0:T(8,128)(2,1)} %hidden_ref.1, ...), custom_call_target="tpu_custom_call" | custom-call | tf_op jit(solution)/shard_map/pallas_call | solution.py:356
  144.2 3.1 %copy.10 = bf16[1,2,128,4096]{3,2,1,0:T(8,128)(2,1)} copy(bf16[1,2,128,4096]{3,2,1,0:T(8,128)(2,1)} %shard_map.82) | data formatting | bytes 4194304
  (3 shorter events, 0.0 us)

commit v2 on v1

--- a/solution.py
+++ b/solution.py
@@ -3,6 +3,7 @@
 
 import jax
 import jax.numpy as jnp
+import numpy as np
 from jax import lax
 from jax.experimental import pallas as pl
 from jax.experimental.pallas import tpu as pltpu
@@ -13,7 +14,7 @@
 HD = 128
 SPAN = 64
 RATIO = HQ // HK
-TILE_HEADS = 4
+TILE_HEADS = 2
 HIDDEN_AWAY = -1e30
 ROPE_BASE = 500000.0
 MESH = pl.DeviceIdType.MESH
@@ -24,7 +25,9 @@
     z_size,
     x_size,
     span_ref,
-    rows_ref,
+    tree_ref,
+    branch_ref,
+    packed_ref,
     inverse_ref,
     gain_ref,
     hidden_ref,
@@ -58,7 +61,7 @@
     z = me // x_size
     x = me % x_size
     micro, _, rows, chunk = state.shape
-    seq_len = rows_ref.shape[2]
+    seq_len = tree_ref.shape[1]
     spans = rows // SPAN
     width = HK * chunk
 
@@ -128,9 +131,9 @@
             offset = span_ref[mb, me * spans + k] * SPAN
             position = position + jnp.where(place // SPAN == k, offset, 0)
         position = position.astype(jnp.float32)
-        tree_row = rows_ref[mb, 0:1, :]
-        branch_row = rows_ref[mb, 1:2, :]
-        packed_row = rows_ref[mb, 2:3, :]
+        tree_row = tree_ref[mb : mb + 1, :].astype(jnp.float32)
+        branch_row = branch_ref[mb : mb + 1, :].astype(jnp.float32)
+        packed_row = packed_ref[mb : mb + 1, :].astype(jnp.float32)
         code_row = tree_row * 3.0 + branch_row
         here = ids == position
         code = jnp.sum(jnp.where(here, code_row, 0.0), axis=1, keepdims=True)
@@ -345,10 +348,9 @@
     chunk = width // HK
     within = jnp.arange(SPAN, dtype=jnp.int32)
     packed = (span_order[:, :, None] * SPAN + within).reshape(micro, seq_len)
-    stacked = jnp.stack([tree_ids, branch_ids, packed], axis=1).astype(jnp.float32)
-    exponent = jnp.arange(HD // 2, dtype=jnp.float32) * (2.0 / HD)
-    inverse = jnp.power(jnp.float32(ROPE_BASE), -exponent)
-    inverse = jnp.concatenate([inverse, inverse])[None]
+    exponent = np.arange(HD // 2, dtype=np.float32) * np.float32(2.0 / HD)
+    inverse = np.power(np.float32(ROPE_BASE), -exponent).astype(np.float32)
+    inverse = jnp.asarray(np.concatenate([inverse, inverse])[None])
     vmem = pl.BlockSpec(memory_space=pltpu.VMEM)
     anywhere = pl.BlockSpec(memory_space=pl.ANY)
     half = jnp.bfloat16
@@ -356,7 +358,7 @@
     return pl.pallas_call(
         functools.partial(kernel, sections, z_size, x_size),
         out_shape=jax.ShapeDtypeStruct((1, micro, rows, width), half),
-        in_specs=[pl.BlockSpec(memory_space=pltpu.SMEM)] + [vmem] * 3 + [anywhere] * 4,
+        in_specs=[pl.BlockSpec(memory_space=pltpu.SMEM)] + [vmem] * 5 + [anywhere] * 4,
         out_specs=anywhere,
         scratch_shapes=[
             pltpu.VMEM((micro, HK, rows, chunk), half),
@@ -383,7 +385,7 @@
         compiler_params=pltpu.CompilerParams(
             collective_id=0, has_side_effects=True, vmem_limit_bytes=56 * 1024 * 1024
         ),
-    )(span_order, stacked, inverse, gain, hidden, queries, key_weight, value_weight)
+    )(span_order, tree_ids, branch_ids, packed, inverse, gain, hidden, queries, key_weight, value_weight)
 
 
 def solution(mesh):

time: 148 us -> 144 us (0.973)
  Pallas kernels: 141 us -> 139 us
    pallas_call x1, Pallas kernels: 141 us -> 139 us  [local(): pl.pallas_call(functools.partial(kernel, sections, z_size, x_size), out_s...]
where the time goes in v2:
time: 144 us; the launch traced here: 143 us
  Pallas kernels  139 us (97%)
  local copies, waits for them, and re-layouts  3.36 us (2%)
    pallas_call x1, Pallas kernels, local(): pl.pallas_call(functools.partial(kernel, sections, z_size, x_size), out_s...  139 us
    unnamed x1, local copies, waits for them, and re-layouts  3.13 us

profile of v2, /device:TPU:29, one launch (start us, length us, event | category | flops | bytes accessed | tf_op | source)
XLA Modules:
  0.0 143.4 jit_solution(6818710137162456424)
XLA Ops:
  0.0 0.7 broadcast_multiply_fusion
  0.7 0.1 add.23
  0.8 0.1 add.20
  0.8 0.1 add.21
  0.9 0.6 broadcast_add_fusion.packed_ref
  1.5 138.7 %shard_map.91 = bf16[1,2,128,4096]{3,2,1,0:T(8,128)(2,1)} custom-call(s32[2,16]{1,0:T(2,128)} %span_ref.1, s32[2,1024]{1,0:T(2,128)} %tree_ref.1, s32[2,1024]{1,0:T(2,128)} %branch_ref.1, s32[2,1024]{1,0:T(2,128)} %broadcast_add_fusion.packed_ref, f32[1,128]{1,0:T(1,128)} %constant.4.clone.inverse_ref, f32[1,4096]{1,0:T(1,128)} %gain_ref.1, ...), custom_call_target="tpu_custom_call" | custom-call | tf_op jit(solution)/shard_map/pallas_call | solution.py:358
  140.3 3.1 %copy.11 = bf16[1,2,128,4096]{3,2,1,0:T(8,128)(2,1)} copy(bf16[1,2,128,4096]{3,2,1,0:T(8,128)(2,1)} %shard_map.91) | data formatting | bytes 4194304
  (1 shorter events, 0.0 us)

commit v3 on v2

--- a/solution.py
+++ b/solution.py
@@ -125,7 +125,7 @@
     def count(flags):
         return jnp.sum(jnp.where(flags, 1.0, 0.0), axis=1, keepdims=True)
 
-    for mb in range(micro):
+    def prepare(mb):
         position = place % SPAN
         for k in range(spans):
             offset = span_ref[mb, me * spans + k] * SPAN
@@ -300,8 +300,12 @@
 
         lax.fori_loop(0, HK, group, 0)
 
+    prepare(0)
+
     @pl.when(section > 0)
     def _():
+        for mb in range(1, micro):
+            prepare(mb)
         for mb in range(micro):
             turn_queries(mb)
 
@@ -310,6 +314,7 @@
     @pl.when(section == 0)
     def _():
         for mb in range(1, micro):
+            prepare(mb)
             project(mb, False)
         for mb in range(micro):
             turn_queries(mb)

time: 144 us -> 144 us (level)
  no operation moved by 1% of the time
where the time goes in v3:
time: 144 us; the launch traced here: 143 us
  Pallas kernels  139 us (97%)
  local copies, waits for them, and re-layouts  3.36 us (2%)
    pallas_call x1, Pallas kernels, local(): pl.pallas_call(functools.partial(kernel, sections, z_size, x_size), out_s...  139 us
    unnamed x1, local copies, waits for them, and re-layouts  3.13 us

profile of v3, /device:TPU:29, one launch (start us, length us, event | category | flops | bytes accessed | tf_op | source)
XLA Modules:
  0.0 143.4 jit_solution(4859564815161943741)
XLA Ops:
  0.0 0.7 broadcast_multiply_fusion
  0.7 0.1 add.23
  0.8 0.1 add.20
  0.8 0.1 add.21
  0.9 0.6 broadcast_add_fusion.packed_ref
  1.5 138.8 %shard_map.91 = bf16[1,2,128,4096]{3,2,1,0:T(8,128)(2,1)} custom-call(s32[2,16]{1,0:T(2,128)} %span_ref.1, s32[2,1024]{1,0:T(2,128)} %tree_ref.1, s32[2,1024]{1,0:T(2,128)} %branch_ref.1, s32[2,1024]{1,0:T(2,128)} %broadcast_add_fusion.packed_ref, f32[1,128]{1,0:T(1,128)} %constant.4.clone.inverse_ref, f32[1,4096]{1,0:T(1,128)} %gain_ref.1, ...), custom_call_target="tpu_custom_call" | custom-call | tf_op jit(solution)/shard_map/pallas_call | solution.py:363
  140.3 3.1 %copy.11 = bf16[1,2,128,4096]{3,2,1,0:T(8,128)(2,1)} copy(bf16[1,2,128,4096]{3,2,1,0:T(8,128)(2,1)} %shard_map.91) | data formatting | bytes 4194304
  (1 shorter events, 0.0 us)
